TPU v7x, 128 devices: a whole 4x4x4 slice. The times are simulated.
128 devices in a mesh: dp: 8 (over x, core), fsdp: 16 (over y, z).
Axes of the slice: x: 4, y: 4, z: 4, core: 2. Of those that a mesh axis runs over, the one named last changes fastest.
Arguments:
- latents: bfloat16 [256, 512, 512], P(('dp', 'fsdp')), may hold values from -6 to 6
- task_ids: int32 [256], P(('dp', 'fsdp')), may hold values from 0 to 17
- slot_counts: int32 [256], P(('dp', 'fsdp')), may hold values from 128 to 512, as said below
- cotangent: bfloat16 [256, 512, 512], P(('dp', 'fsdp')), may hold values from -6 to 6
- task_embed: bfloat16 [18, 512], P(None, ('dp', 'fsdp')), may hold values from -3 to 3
- norms: bfloat16 [4, 512], P(None, ('dp', 'fsdp')), may hold values from 0.5 to 1.5
- attn_in: bfloat16 [512, 1536], P(('dp', 'fsdp')), may hold values from -0.25 to 0.25
- attn_out: bfloat16 [512, 512], P(('dp', 'fsdp')), may hold values from -2 to 2
- out_biases: bfloat16 [2, 512], P(None, ('dp', 'fsdp')), may hold values from -2 to 2
- mlp_in: bfloat16 [512, 2048], P(('dp', 'fsdp')), may hold values from -0.25 to 0.25
- mlp_in_bias: bfloat16 [2048], P(('dp', 'fsdp')), may hold values from -3 to 3
- mlp_out: bfloat16 [2048, 512], P(('dp', 'fsdp')), may hold values from -0.125 to 0.125
Outputs:
- latents_out: bfloat16 [256, 512, 512], P(('dp', 'fsdp'))
- grad_latents: bfloat16 [256, 512, 512], P(('dp', 'fsdp'))
- grad_task_embed: float32 [18, 512], P(None, ('dp', 'fsdp'))
- grad_norms: float32 [4, 512], P(None, ('dp', 'fsdp'))
- grad_attn_in: float32 [512, 1536], P(('dp', 'fsdp'))
- grad_attn_out: float32 [512, 512], P(('dp', 'fsdp'))
- grad_out_biases: float32 [2, 512], P(None, ('dp', 'fsdp'))
- grad_mlp_in: float32 [512, 2048], P(('dp', 'fsdp'))
- grad_mlp_in_bias: float32 [2048], P(('dp', 'fsdp'))
- grad_mlp_out: float32 [2048, 512], P(('dp', 'fsdp'))
Inputs may be any that keep to these rules, and one draw needn't show every extreme that they name: `slot_counts`: some array has exactly 512 valid slots and some has exactly 128.
All inputs are finite; a program needn't handle non-finite values.
Results may differ from a plain program's by a relative error of at most 0.012.
Values may be sent and summed in bfloat16 or wider, within the bound.
A program may use at most 192 MiB of HBM per device.

v0:
```python
import functools
import math

import jax
import jax.numpy as jnp
from jax import lax
from jax.experimental import pallas as pl
from jax.experimental.pallas import tpu as pltpu
from jax.sharding import PartitionSpec as P

HEADS = 8
EPS = 1e-05
BEST = lax.Precision.HIGHEST
MESH = pl.DeviceIdType.MESH
ALL = slice(None)
ORDERS = (("z", "y", "x"), ("y", "x", "z"), ("x", "z", "y"))
TILES = 12
WAVES = (((0, 1), (1, 1), (2, 1)), ((3, 3), (6, 3), (9, 3)))


def my_position():
    dp, fsdp = lax.axis_index("dp"), lax.axis_index("fsdp")
    return {
        "x": lax.div(dp, 2),
        "c": lax.rem(dp, 2),
        "y": lax.div(fsdp, 4),
        "z": lax.rem(fsdp, 4),
    }


def moved(pos, axis, step):
    size = 2 if axis == "c" else 4
    return {**pos, axis: lax.rem(pos[axis] + step, size)}


def device_of(pos):
    return (pos["x"] * 2 + pos["c"], pos["y"] * 4 + pos["z"])


def partners_of(pos):
    return [moved(pos, axis, k) for axis in "xyz" for k in (1, 2, 3)] + [moved(pos, "c", 1)]


def greet(pos):
    barrier = pltpu.get_barrier_semaphore()
    for other in partners_of(pos):
        pl.semaphore_signal(barrier, inc=1, device_id=device_of(other), device_id_type=MESH)


def greeted(pos):
    pl.semaphore_wait(pltpu.get_barrier_semaphore(), 10)


def remote(src, dst, send, recv, pos):
    return pltpu.make_async_remote_copy(
        src_ref=src, dst_ref=dst, send_sem=send, recv_sem=recv,
        device_id=device_of(pos), device_id_type=MESH,
    )


class Gather:
    def __init__(self, wave, own, tiles, send, recv, pos):
        self.wave, self.own, self.tiles, self.pos = wave, own, tiles, pos
        self.send, self.recv = send, recv

    def slab(self, part, free, at=None):
        first, count = WAVES[self.wave][part]
        place = {**self.pos, **(at or {})}
        index = [ALL if axis in free else place[axis] for axis in "xcyz"]
        return self.tiles.at[(pl.ds(first, count), *index)]

    def stage_copy(self, part, stage, k):
        order = ORDERS[part]
        slab = self.slab(part, order[:stage])
        src = slab
        if stage == 0:
            first, count = WAVES[self.wave][part]
            src = self.own.at[pl.ds(first, count)]
        slot = (self.wave, part, stage * 3 + k - 1)
        return remote(src, slab, self.send.at[slot], self.recv.at[slot], moved(self.pos, order[stage], k))

    def pair_copy(self, part, k):
        order = ORDERS[part]
        at = {order[2]: lax.rem(self.pos[order[2]] + 4 - k, 4)} if k else None
        slab = self.slab(part, order[:2], at)
        slot = (self.wave, part, 9 + k)
        return remote(slab, slab, self.send.at[slot], self.recv.at[slot], moved(self.pos, "c", 1))

    def start(self, stage):
        for part in range(3):
            for k in (2, 1, 3):
                self.stage_copy(part, stage, k).start()
            if stage == 2:
                self.pair_copy(part, 0).start()

    def arrive(self, stage):
        for part in range(3):
            for k in (1, 3, 2):
                self.stage_copy(part, stage, k).wait_recv()
                if stage == 2:
                    self.pair_copy(part, k).start()

    def arrive_pair(self, part):
        for k in range(4):
            self.pair_copy(part, k).wait_recv()

    def settle(self):
        for part in range(3):
            for stage in range(3):
                for k in (1, 2, 3):
                    self.stage_copy(part, stage, k).wait_send()
            for k in range(4):
                self.pair_copy(part, k).wait_send()


class SmallGather:
    def __init__(self, own, slots, kept, pair, send, recv, pos):
        self.own, self.slots, self.kept, self.pair = own, slots, kept, pair
        self.send, self.recv, self.pos = send, recv, pos

    def copy(self, stage, k):
        here = self.kept.at[self.pos["x"]]
        src = self.own if stage == 0 else here
        dst = here if stage == 2 else self.slots.at[stage, k - 1]
        slot = stage * 3 + k - 1
        return remote(src, dst, self.send.at[slot], self.recv.at[slot], moved(self.pos, "zyx"[stage], k))

    def pair_copy(self):
        return remote(self.kept, self.pair, self.send.at[9], self.recv.at[9], moved(self.pos, "c", 1))

    def start(self, stage):
        for k in (2, 1, 3):
            self.copy(stage, k).start()

    def arrive(self, stage):
        for k in (1, 3, 2):
            self.copy(stage, k).wait_recv()
        if stage == 2:
            self.pair_copy().start()
            return
        total = self.own[...] if stage == 0 else self.kept[self.pos["x"]]
        if stage == 1:
            for k in (1, 2, 3):
                self.copy(1, k).wait_send()
        for k in range(3):
            total = total + self.slots[stage, k]
        self.kept[self.pos["x"]] = total

    def arrive_pair(self, out):
        self.pair_copy().wait_recv()
        for x in range(4):
            out[:, x * 128 : (x + 1) * 128] = self.kept[x].astype(jnp.float32) + self.pair[x].astype(jnp.float32)

    def settle(self):
        for stage in (0, 2):
            for k in (1, 2, 3):
                self.copy(stage, k).wait_send()
        self.pair_copy().wait_send()


class Piece:
    def __init__(self, r, pos, number, first, count, order, x=None, stages=(0, 1, 2)):
        self.r, self.pos, self.number, self.first, self.count = r, pos, number, first, count
        self.order, self.x, self.stages = order, x, stages

    def span(self):
        return pl.ds(self.first, self.count)

    def pair_copy(self):
        other = moved(self.pos, "c", 1)
        x = ALL if self.x is None else self.x
        return remote(
            self.r.tiles.at[self.span(), x, other["c"]], self.r.from_pair.at[self.span(), x],
            self.r.p_send.at[self.number], self.r.p_recv.at[self.number], other,
        )

    def pair_add(self):
        self.pair_copy().wait_recv()
        core = self.pos["c"]
        for n in range(self.count):
            t = self.first + n
            for x in range(4) if self.x is None else (self.x,):
                total = self.r.tiles[t, x, core].astype(jnp.float32) + self.r.from_pair[t, x].astype(jnp.float32)
                self.r.tiles[t, x, core] = total.astype(jnp.bfloat16)

    def index(self, stage, place):
        held = self.order[: stage + 1]
        found = []
        for axis in "xcyz":
            if axis == "c" or axis in held:
                found.append(place[axis])
            else:
                found.append(self.x if axis == "x" and self.x is not None else ALL)
        return tuple(found)

    def left(self, stage):
        free = [axis for axis in "xyz" if axis not in self.order[: stage + 1]]
        return tuple(self.x if axis == "x" and self.x is not None else ALL for axis in free)

    def copy(self, stage, k):
        axis = self.order[stage]
        other = moved(self.pos, axis, k)
        src = self.r.tiles.at[(self.span(), *self.index(stage, other))]
        dst = (self.r.from1, self.r.from2, self.r.from3)[stage].at[(self.span(), k - 1, *self.left(stage))]
        slot = (self.number, stage * 3 + k - 1)
        return remote(src, dst, self.r.r_send.at[slot], self.r.r_recv.at[slot], other)

    def start(self, stage):
        for k in (2, 1, 3):
            self.copy(stage, k).start()

    def add(self, stage):
        for k in (1, 3, 2):
            self.copy(stage, k).wait_recv()
        index, left = self.index(stage, self.pos), self.left(stage)
        arrived = (self.r.from1, self.r.from2, self.r.from3)[stage]
        for n in range(self.count):
            t = self.first + n
            total = self.r.tiles[(t, *index)].astype(jnp.float32)
            for k in range(3):
                total = total + arrived[(t, k, *left)].astype(jnp.float32)
            if stage == 2:
                self.r.total[t] = total
            else:
                self.r.tiles[(t, *index)] = total.astype(jnp.bfloat16)

    def settle(self):
        if self.number < 12 and self.stages != (0, 1):
            self.pair_copy().wait_send()
        for stage in self.stages:
            for k in (1, 2, 3):
                self.copy(stage, k).wait_send()


class SmallScatter:
    def __init__(self, own, pair, slots, held, send, recv, pos):
        self.own, self.pair, self.slots, self.held = own, pair, slots, held
        self.send, self.recv, self.pos = send, recv, pos

    def pair_copy(self):
        return remote(self.own, self.pair, self.send.at[9], self.recv.at[9], moved(self.pos, "c", 1))

    def copy(self, stage, k):
        other = moved(self.pos, "xyz"[stage], k)
        src = self.held.at[other["x"]] if stage == 0 else self.held.at[3 + stage]
        slot = stage * 3 + k - 1
        return remote(src, self.slots.at[stage, k - 1], self.send.at[slot], self.recv.at[slot], other)

    def add_pair(self):
        self.pair_copy().wait_recv()
        self.held[0:4] = self.own[...] + self.pair[...]

    def start(self, stage):
        for k in (2, 1, 3):
            self.copy(stage, k).start()

    def add(self, stage):
        for k in (1, 3, 2):
            self.copy(stage, k).wait_recv()
        total = self.held[self.pos["x"]] if stage == 0 else self.held[3 + stage]
        for k in range(3):
            total = total + self.slots[stage, k]
        self.held[4 + stage] = total

    def settle(self):
        self.pair_copy().wait_send()
        for stage in range(3):
            for k in (1, 2, 3):
                self.copy(stage, k).wait_send()


COLUMNS = (
    (0, 4, 8, 1),
    (5, 9, 2, 6),
    (10, 3, 7, 11),
    (0, 1, 2, 3),
    *(tuple(range(4 * j, 4 * j + 4)) for j in range(4)),
)


def quarter_order(transposed=False):
    a = lax.broadcasted_iota(jnp.int32, (256, 256), 1 if transposed else 0)
    b = lax.broadcasted_iota(jnp.int32, (256, 256), 0 if transposed else 1)
    source = ((a % 64) // 4) * 16 + (a // 64) * 4 + a % 4
    return (source == b).astype(jnp.float32).astype(jnp.bfloat16)


def unfold(r, t, out):
    blocks = [r.tiles[t, xc // 2, xc % 2].reshape(256, 128) for xc in range(8)]
    rows = nn(quarter_order(), jnp.concatenate(blocks, 1)).astype(jnp.bfloat16)
    for q, ct in enumerate(COLUMNS[t]):
        for xc in range(8):
            out[xc * 64 : (xc + 1) * 64, ct * 128 : (ct + 1) * 128] = rows[q * 64 : (q + 1) * 64, xc * 128 : (xc + 1) * 128]


def unfold_plain(r, out):
    def one(i):
        x, c = lax.div(i, 2), lax.rem(i, 2)
        for t in range(4):
            out[pl.ds(pl.multiple_of(i * 256, 256), 256), t * 128 : (t + 1) * 128] = r.tiles[8 + t, x, c].reshape(256, 128)

    loop(8, one)


def fold(r, columns, t):
    rows = [jnp.concatenate([block[xc * 64 : (xc + 1) * 64] for xc in range(8)], 1) for block in columns]
    blocks = nn(quarter_order(True), jnp.concatenate(rows, 0)).astype(jnp.bfloat16)
    for xc in range(8):
        r.tiles[t, xc // 2, xc % 2] = blocks[:, xc * 128 : (xc + 1) * 128].reshape(4, 4, 16, 128)


def small_place(pos):
    ring = pos["y"] * 4 + pos["z"]
    return pos["c"] * 64 + ring * 4, 24 + pos["c"] * 2 + lax.div(ring, 8), 16 * lax.rem(ring, 8)


F32, BF16 = jnp.float32, jnp.bfloat16
GELU0 = math.sqrt(2.0 / math.pi)
GELU1 = GELU0 * 0.044715


def nn(a, b):
    return jnp.dot(a, b, preferred_element_type=F32)


def nt(a, b):
    return lax.dot_general(a, b, (((1,), (1,)), ((), ())), preferred_element_type=F32)


def tn(a, b):
    return lax.dot_general(a, b, (((0,), (0,)), ((), ())), preferred_element_type=F32)


def span_of(n, size):
    if isinstance(n, int):
        return slice(n * size, (n + 1) * size)
    return pl.ds(pl.multiple_of(n * size, size), size)


def rows_of(i):
    return span_of(i, 512)


def normalized(h):
    centred = h - jnp.mean(h, axis=-1, keepdims=True)
    factor = lax.rsqrt(jnp.mean(centred * centred, axis=-1, keepdims=True) + EPS)
    return centred * factor, factor


def normalized_back(grad, unit, factor, gain):
    scaled = grad * gain
    inner = jnp.mean(scaled, axis=-1, keepdims=True)
    along = jnp.mean(scaled * unit, axis=-1, keepdims=True)
    return factor * (scaled - inner - unit * along)


def column_sum(v):
    return jnp.sum(v, axis=0, keepdims=True)


def embedding(r, i):
    row = lax.broadcasted_iota(jnp.int32, (24, 1), 0)
    return column_sum(jnp.where(row == r.task_ids[i], r.params[0:24], 0.0))


def head_lanes(h):
    lane = lax.broadcasted_iota(jnp.int32, (1, 128), 1)
    return ((lane >= 64) == (h == 1)).astype(F32).astype(BF16)


def first_norm(r, i):
    unit, factor = normalized(r.lat[i].astype(F32) + embedding(r, i))
    r.a1[rows_of(i)] = (unit * r.params[18:19] + r.params[19:20]).astype(BF16)
    r.u1[rows_of(i)] = unit
    r.factors[rows_of(i), 0:1] = factor


def project(r, i):
    a1 = r.a1[rows_of(i)]
    for part in range(3):
        columns = slice(part * 512, (part + 1) * 512)
        result = nn(a1, r.w_qkv[:, columns])
        if part == 0:
            result = result * 0.125
        r.qkv[rows_of(i), columns] = result.astype(BF16)


def pair_of(r, i, hp, part):
    return r.qkv[rows_of(i), span_of(part * 4 + hp, 128)]


def attend(r, i, hp):
    q, k, v = (pair_of(r, i, hp, part) for part in range(3))
    slots = lax.broadcasted_iota(jnp.int32, (1, 512), 1)
    bias = jnp.where(slots < r.counts[i], 0.0, -1000000000.0)
    mixed = None
    for h in range(2):
        lanes = head_lanes(h)
        scores = nt(q, k * lanes) + bias
        expo = jnp.exp(scores - jnp.max(scores, axis=-1, keepdims=True)).astype(BF16)
        r.expo[i * 8 + hp * 2 + h] = expo
        wide = jnp.concatenate((v * lanes, jnp.broadcast_to(lanes, (512, 128))), 1)
        term = nn(expo, wide)
        mixed = term if mixed is None else mixed + term
    inverse = 1.0 / mixed[:, 128:]
    columns = span_of(hp, 128)
    r.inverse[rows_of(i), columns] = inverse
    mean = mixed[:, :128] * inverse
    r.o32[rows_of(i), columns] = mean
    r.o[rows_of(i), columns] = mean.astype(BF16)


def second_norm(r, i):
    h1 = r.lat[i].astype(F32) + embedding(r, i) + (nn(r.o[rows_of(i)], r.w_out[...]) + r.params[22:23])
    unit, factor = normalized(h1)
    r.a2[rows_of(i)] = (unit * r.params[20:21] + r.params[21:22]).astype(BF16)
    r.u2[rows_of(i)] = unit
    r.factors[rows_of(i), 1:2] = factor
    r.result[rows_of(i)] = h1


def feed_forward(r, j):
    units, tile = span_of(j, 512), span_of(j, 128)
    bias = jnp.concatenate([r.params[24 + m : 25 + m, tile] for m in range(4)], 1)
    sums = None
    for i in range(2):
        z = nn(r.a2[rows_of(i)], r.w_up[:, units]) + bias
        z2 = z * z
        half = 0.5 + 0.5 * jnp.tanh(z * (GELU0 + GELU1 * z2))
        act = (z * half).astype(BF16)
        slope = half + z * (2 * GELU0 + 6 * GELU1 * z2) * (half * (1.0 - half))
        gz = (nt(r.y[i], r.w_down[units, :]) * slope).astype(BF16)
        r.act[rows_of(i), units] = act
        r.gz[j % 2, rows_of(i)] = gz
        back = nt(gz, r.w_up[:, units])
        r.back[rows_of(i)] = back if isinstance(j, int) and j == 0 else r.back[rows_of(i)] + back
        total = column_sum(gz.astype(F32))
        sums = total if sums is None else sums + total
    for m in range(4):
        r.small[j, 24 + m : 25 + m] = sums[:, m * 128 : (m + 1) * 128]


def chunk_gradients(r, j):
    g_down = tn(r.act[:, span_of(j, 512)], r.y[...].reshape(1024, 512)).astype(BF16)
    for c in range(2):
        for t in range(4):
            r.tiles[8 + t, j, c] = g_down[c * 256 : (c + 1) * 256, t * 128 : (t + 1) * 128].reshape(4, 4, 16, 128)
    g_up = tn(r.a2[...], r.gz[j % 2]).astype(BF16)
    fold(r, [g_up[:, q * 128 : (q + 1) * 128] for q in range(4)], 4 + j)


def add_small(r, row, value):
    for x in range(4):
        r.small[x, row : row + 1] = r.small[x, row : row + 1] + value[:, x * 128 : (x + 1) * 128]


def second_norm_back(r, i):
    grad, unit = r.back[rows_of(i)], r.u2[rows_of(i)]
    add_small(r, 20, column_sum(grad * unit))
    add_small(r, 21, column_sum(grad))
    y = r.y[i].astype(F32)
    add_small(r, 23, column_sum(y))
    gh1 = y + normalized_back(grad, unit, r.factors[rows_of(i), 1:2], r.params[20:21])
    r.back[rows_of(i)] = gh1
    gb = gh1.astype(BF16)
    r.gb[rows_of(i)] = gb
    add_small(r, 22, column_sum(gb.astype(F32)))
    go = (nt(gb, r.w_out[...]) * r.inverse[rows_of(i)]).astype(BF16)
    r.go[rows_of(i)] = go
    product = go.astype(F32) * r.o32[rows_of(i)]
    high = product.astype(BF16).astype(F32)
    low = product - high
    first = lax.broadcasted_iota(jnp.int32, (1, 128), 1) < 64
    for hp in range(4):
        columns = slice(hp * 128, (hp + 1) * 128)
        swapped = pltpu.roll(low[:, columns], 64, 1)
        r.god0[rows_of(i), columns] = jnp.where(first, high[:, columns], swapped).astype(BF16)
        r.god1[rows_of(i), columns] = jnp.where(first, swapped, high[:, columns]).astype(BF16)


def out_gradient(r):
    g_out = tn(r.o[...], r.gb[...]).astype(BF16)
    fold(r, [g_out[:, q * 128 : (q + 1) * 128] for q in range(4)], 3)


def result_of(r, i):
    r.out[i] = (r.result[rows_of(i)] + nn(r.act[rows_of(i)], r.w_down[...]) + r.params[23:24]).astype(BF16)


def attend_back(r, i, hp):
    q, k, v = (pair_of(r, i, hp, part) for part in range(3))
    columns = span_of(hp, 128)
    go = r.go[rows_of(i), columns]
    gq = gk = gv = 0.0
    for h in range(2):
        lanes = head_lanes(h)
        both = jnp.concatenate((go, (r.god0, r.god1)[h][rows_of(i), columns]), 1)
        wide = jnp.concatenate((v * lanes, jnp.full((512, 128), -1.0, BF16)), 1)
        expo = r.expo[i * 8 + hp * 2 + h]
        gs = (expo.astype(F32) * nt(both, wide)).astype(BF16)
        gq = gq + nn(gs, k * lanes)
        gk = gk + tn(gs, q * lanes)
        gv = gv + tn(expo, go * lanes)
    for part, value in enumerate((gq * 0.125, gk, gv)):
        r.gqkv[i][part][:, span_of(hp, 128)] = value.astype(BF16)


def first_norm_back(r, i):
    grad, unit = nt(jnp.concatenate([part[...] for part in r.gqkv[i]], 1), r.w_qkv[...]), r.u1[rows_of(i)]
    add_small(r, 18, column_sum(grad * unit))
    add_small(r, 19, column_sum(grad))
    gh0 = r.back[rows_of(i)] + normalized_back(grad, unit, r.factors[rows_of(i), 0:1], r.params[18:19])
    r.glat[i] = gh0.astype(BF16)
    total = column_sum(gh0)
    row = lax.broadcasted_iota(jnp.int32, (18, 1), 0)
    for x in range(4):
        mine = jnp.where(row == r.task_ids[i], total[:, x * 128 : (x + 1) * 128], 0.0)
        r.small[x, 0:18] = r.small[x, 0:18] + mine


def in_gradient(r, t):
    columns = jnp.concatenate(
        [jnp.concatenate([r.gqkv[i][ct // 4][:, span_of(ct % 4, 128)] for ct in COLUMNS[t]], 1) for i in range(2)]
    )
    g_in = tn(r.a1[...], columns).astype(BF16)
    fold(r, [g_in[:, q * 128 : (q + 1) * 128] for q in range(4)], t)


class Refs:
    def __init__(self, names, refs):
        for name, ref in zip(names, refs, strict=True):
            setattr(self, name, ref)


RAW = {
    "raw_in": ((4, 1536), BF16),
    "raw_out": ((4, 512), BF16),
    "raw_up": ((4, 2048), BF16),
    "raw_down": ((16, 512), BF16),
    "raw_table": ((4, 18), BF16),
    "raw_norms": ((4, 4), BF16),
    "raw_biases": ((2, 4), BF16),
    "raw_up_bias": ((1, 16), BF16),
}
INPUTS = ("task_ids", "counts", "lat_hbm", "y_hbm", *(f"{name}_hbm" for name in RAW))
OUTPUTS = ("out_hbm", "glat_hbm", "total", "s_total")
BLOCKS = (TILES, 4, 2, 4, 4, 16, 128)
SCRATCH = {
    **RAW,
    "own32": ((TILES, 16, 128), F32),
    "own": ((TILES, 16, 128), BF16),
    "small32": ((40, 128), F32),
    "table32": ((128, 128), F32),
    "own_small": ((32, 128), BF16),
    "lat": ((2, 512, 512), BF16),
    "y": ((2, 512, 512), BF16),
    "w_qkv": ((512, 1536), BF16),
    "w_out": ((512, 512), BF16),
    "w_up": ((512, 2048), BF16),
    "w_down": ((2048, 512), BF16),
    "params": ((32, 512), F32),
    "a1": ((1024, 512), BF16),
    "u1": ((1024, 512), F32),
    "qkv": ((1024, 1536), BF16),
    "expo": ((16, 512, 512), BF16),
    "o": ((1024, 512), BF16),
    "o32": ((1024, 512), F32),
    "inverse": ((1024, 512), F32),
    "result": ((1024, 512), F32),
    "a2": ((1024, 512), BF16),
    "u2": ((1024, 512), F32),
    "factors": ((1024, 2), F32),
    "act": ((1024, 2048), BF16),
    "gz": ((2, 1024, 512), BF16),
    "back": ((1024, 512), F32),
    "gb": ((1024, 512), BF16),
    "small": ((4, 32, 128), F32),
    "tiles": (BLOCKS, BF16),
    "slots": ((2, 3, 32, 128), BF16),
    "kept": ((4, 32, 128), BF16),
    "pair": ((4, 32, 128), BF16),
    "from_pair": ((TILES, 4, 4, 4, 16, 128), BF16),
    "from1": ((TILES, 3, 4, 4, 16, 128), BF16),
    "from2": ((TILES, 3, 4, 16, 128), BF16),
    "from3": ((TILES, 3, 16, 128), BF16),
    "s_pair": ((4, 32, 128), F32),
    "s_slots": ((3, 3, 32, 128), F32),
    "s_held": ((7, 32, 128), F32),
}
SEMAPHORES = {
    "g_send": (2, 3, 13),
    "g_recv": (2, 3, 13),
    "gs_send": (10,),
    "gs_recv": (10,),
    "p_send": (12,),
    "p_recv": (12,),
    "r_send": (17, 9),
    "r_recv": (17, 9),
    "rs_send": (10,),
    "rs_recv": (10,),
    "local": (12,),
}


def alias(r):
    r.go, r.god0, r.god1 = r.gz.at[0], r.gz.at[1], r.a2
    r.out, r.glat = r.lat, r.y
    r.gqkv = [r.w_up.at[:, span_of(part, 512)] for part in range(3)], [r.lat.at[0], r.lat.at[1], r.w_out]


def loop(count, step):
    lax.fori_loop(0, count, lambda n, carry: (step(n), carry)[1], 0)


def pack_own(r, pos):
    for t, blocks in enumerate(COLUMNS):
        raw = (r.raw_in, r.raw_out, r.raw_up)[0 if t < 3 else 1 if t == 3 else 2]
        for q, ct in enumerate(blocks):
            r.own32[t, 4 * q : 4 * q + 4] = raw[:, ct * 128 : (ct + 1) * 128].astype(F32)
    for t in range(8):
        r.own[t] = r.own32[t].astype(BF16)
    for t in range(4):
        r.own[8 + t] = r.raw_down[:, t * 128 : (t + 1) * 128]
    r.small32[...] = jnp.zeros_like(r.small32)
    r.table32[...] = jnp.zeros_like(r.table32)
    r.table32[0:4, 0:18] = r.raw_table[...].astype(F32)
    r.small32[18:22, 0:4] = r.raw_norms[...].astype(F32)
    r.small32[22:24, 0:4] = r.raw_biases[...].astype(F32)
    r.small32[32:33, 0:16] = r.raw_up_bias[...].astype(F32)
    offset, bias_row, bias_offset = small_place(pos)
    block = pltpu.roll(r.small32[0:32] + r.table32[...].T[0:32], offset, 1)
    bias = pltpu.roll(r.small32[32:40], bias_offset, 1)[0:1]
    row = lax.broadcasted_iota(jnp.int32, (32, 1), 0)
    r.own_small[...] = (block + jnp.where(row == bias_row, bias, 0.0)).astype(BF16)


def kernel(*refs):
    r = Refs((*INPUTS, *OUTPUTS, *SCRATCH, *SEMAPHORES), refs)
    alias(r)
    pos = my_position()
    loads = [
        pltpu.make_async_copy(getattr(r, f"{name}_hbm"), getattr(r, name), r.local.at[n])
        for n, name in enumerate((*RAW, "lat", "y"))
    ]
    store_out = pltpu.make_async_copy(r.out, r.out_hbm, r.local.at[10])
    store_glat = pltpu.make_async_copy(r.glat, r.glat_hbm, r.local.at[11])
    greet(pos)
    for load in loads:
        load.start()
    gathers = [Gather(w, r.own, r.tiles, r.g_send, r.g_recv, pos) for w in range(2)]
    tiny = SmallGather(r.own_small, r.slots, r.kept, r.pair, r.gs_send, r.gs_recv, pos)
    tiny_sum = SmallScatter(r.small, r.s_pair, r.s_slots, r.s_held, r.rs_send, r.rs_recv, pos)
    g_in = [Piece(r, pos, t, t, 1, ORDERS[t][::-1]) for t in range(3)]
    g_out = Piece(r, pos, 3, 3, 1, ("x", "z", "y"))
    down_orders = (("z", "y", "x"), ("y", "z", "x"))

    def chunk(j):
        up = Piece(r, pos, 4 + j, 4 + j, 1, ("x", "y", "z"))
        down = Piece(r, pos, 8 + j, 8, 4, (), x=j, stages=())
        halves = [Piece(r, pos, 8 + 2 * j + n, 8 + 2 * n, 2, down_orders[n], x=j, stages=(0, 1)) for n in range(2)]
        return up, down, halves

    chunks = [chunk(j) for j in range(4)]
    g_up, g_down, g_halves = zip(*chunks, strict=True)
    g_last = Piece(r, pos, 16, 8, 4, ("z", "y", "x"), stages=(2,))
    for load in loads[:8]:
        load.wait()
    pack_own(r, pos)
    greeted(pos)

    gathers[0].start(0)
    tiny.start(0)
    gathers[1].start(0)
    for t in range(TILES):
        r.tiles[t, pos["x"], pos["c"], pos["y"], pos["z"]] = r.own[t]
    r.small[...] = jnp.zeros_like(r.small)
    gathers[0].arrive(0)
    gathers[0].start(1)
    tiny.arrive(0)
    tiny.start(1)
    gathers[1].arrive(0)
    gathers[1].start(1)
    gathers[0].arrive(1)
    gathers[0].start(2)
    tiny.arrive(1)
    tiny.start(2)
    tiny.arrive(2)
    gathers[0].arrive(2)
    gathers[1].arrive(1)
    gathers[1].start(2)
    tiny.arrive_pair(r.params)
    loads[8].wait()
    for i in range(2):
        first_norm(r, i)
    for t in range(3):
        gathers[0].arrive_pair(t)
    for t in range(3):
        unfold(r, t, r.w_qkv)
    for i in range(2):
        project(r, i)

    def forward(i):
        for hp in range(4):
            attend(r, i, hp)

    loop(2, forward)
    gathers[1].arrive(2)
    gathers[1].arrive_pair(0)
    unfold(r, 3, r.w_out)
    for i in range(2):
        second_norm(r, i)
    for part in (1, 2):
        gathers[1].arrive_pair(part)
    for t in range(4, 8):
        unfold(r, t, r.w_up)
    unfold_plain(r, r.w_down)
    for gather in gathers:
        gather.settle()
    tiny.settle()
    loads[9].wait()

    def leave(j):
        up, down, _ = chunk(j)
        up.pair_copy().start()
        down.pair_copy().start()

    def begin(j):
        up, down, halves = chunk(j)
        up.pair_add()
        down.pair_add()
        for piece in (up, *halves):
            piece.start(0)

    def turn(piece, stage):
        piece.add(stage)
        piece.start(stage + 1)

    def second(j):
        for piece in (g_up[j], *g_halves[j]):
            turn(piece, 0)

    def third(j):
        turn(g_up[j], 1)
        for piece in g_halves[j]:
            piece.add(1)

    feed_forward(r, 0)

    def middle(n):
        feed_forward(r, n + 1)
        chunk_gradients(r, n)
        leave(n)

        @pl.when(n > 0)
        def _():
            begin(n - 1)

    loop(3, middle)
    chunk_gradients(r, 3)
    leave(3)
    begin(2)
    second(0)
    second_norm_back(r, 0)
    second_norm_back(r, 1)
    begin(3)
    second(1)
    out_gradient(r)
    g_out.pair_copy().start()

    def backward(half):
        for n in range(4):
            attend_back(r, n % 2, half * 2 + n // 2)

        @pl.when(half == 0)
        def _():
            g_out.pair_add()
            g_out.start(0)
            second(2)
            third(0)
            in_gradient(r, 0)
            g_in[0].pair_copy().start()
            second(3)
            third(1)

    loop(2, backward)
    in_gradient(r, 1)
    g_in[1].pair_copy().start()
    g_in[0].pair_add()
    g_in[0].start(0)
    turn(g_out, 0)
    third(2)
    in_gradient(r, 2)
    g_in[2].pair_copy().start()
    g_in[1].pair_add()
    g_in[1].start(0)
    third(3)
    g_last.start(2)
    first_norm_back(r, 0)
    g_in[2].pair_add()
    g_in[2].start(0)
    first_norm_back(r, 1)
    tiny_sum.pair_copy().start()
    store_glat.start()
    turn(g_in[0], 0)
    turn(g_out, 1)
    tiny_sum.add_pair()
    tiny_sum.start(0)
    result_of(r, 0)
    result_of(r, 1)
    store_out.start()
    tiny_sum.add(0)
    tiny_sum.start(1)
    turn(g_in[2], 0)
    turn(g_in[1], 0)
    turn(g_in[0], 1)
    for piece in (*g_up, g_last):
        piece.add(2)
    tiny_sum.add(1)
    tiny_sum.start(2)
    turn(g_in[2], 1)
    turn(g_in[1], 1)
    g_out.add(2)
    g_in[0].add(2)
    for piece in (*g_in, g_out, *g_up, *g_down, *(half for halves in g_halves for half in halves), g_last):
        piece.settle()
    store_out.wait()
    store_glat.wait()
    g_in[1].add(2)
    g_in[2].add(2)
    tiny_sum.add(2)
    r.s_total[...] = r.s_held[6]
    tiny_sum.settle()


SHAPES = ((4, 18), (4, 4), (4, 1536), (4, 512), (2, 4), (4, 2048), (1, 16), (16, 512))


def finish(*refs):
    out_in, glat_in, total_hbm, small_hbm, out, glat, *rest = refs
    targets, (held, total, small), parts, (sems, load_sems, store_sems) = rest[:8], rest[8:11], rest[11:19], rest[19:]
    table, norms, w_in, w_out, biases, w_up, up_bias, w_down = parts
    loads = [
        pltpu.make_async_copy(total_hbm, total, load_sems.at[0]),
        pltpu.make_async_copy(small_hbm, small, load_sems.at[1]),
    ]
    for load in loads:
        load.start()
    reads, writes = [], []
    for n, (source, target) in enumerate(((out_in, out), (glat_in, glat))):
        for k in range(4):
            slot, rows = 4 * n + k, pl.ds(k % 2 * 256, 256)
            reads.append(pltpu.make_async_copy(source.at[k // 2, rows], held.at[slot], sems.at[0, slot]))
            writes.append(pltpu.make_async_copy(held.at[slot], target.at[k // 2, rows], sems.at[1, slot]))
    for read in reads:
        read.start()
    for load in loads:
        load.wait()
    for t, blocks in enumerate(COLUMNS):
        to = (w_in, w_out, w_up)[0 if t < 3 else 1 if t == 3 else 2]
        for q, ct in enumerate(blocks):
            to[:, ct * 128 : (ct + 1) * 128] = total[t, 4 * q : 4 * q + 4]
    for t in range(4):
        w_down[:, t * 128 : (t + 1) * 128] = total[8 + t]
    offset, bias_row, bias_offset = small_place(my_position())
    block = pltpu.roll(small[...], lax.rem(128 - offset, 128), 1)
    table[...] = jnp.concatenate((block, jnp.zeros((96, 128), F32))).T[0:4, 0:18]
    norms[...] = block[18:22, 0:4]
    biases[...] = block[22:24, 0:4]
    row = lax.broadcasted_iota(jnp.int32, (32, 1), 0)
    bias = jnp.sum(jnp.where(row == bias_row, small[...], 0.0), axis=0, keepdims=True)
    bias = pltpu.roll(jnp.broadcast_to(bias, (8, 128)), lax.rem(128 - bias_offset, 128), 1)
    up_bias[...] = bias[0:1, 0:16]
    stores = [
        pltpu.make_async_copy(part, target, store_sems.at[n])
        for n, (part, target) in enumerate(zip(parts, targets, strict=True))
    ]
    for store in stores:
        store.start()
    for read, write in zip(reads, writes, strict=True):
        read.wait()
        write.start()
    for copy in (*stores, *writes):
        copy.wait()


def whole(task_ids, counts, latents, cotangent, *raw):
    vmem = pl.BlockSpec(memory_space=pltpu.VMEM)
    smem = pl.BlockSpec(memory_space=pltpu.SMEM)
    hbm = pl.BlockSpec(memory_space=pl.ANY)
    array = jax.ShapeDtypeStruct(latents.shape, BF16)
    found = pl.pallas_call(
        kernel,
        out_shape=[
            array,
            array,
            jax.ShapeDtypeStruct((TILES, 16, 128), F32),
            jax.ShapeDtypeStruct((32, 128), F32),
        ],
        in_specs=[smem, smem] + [hbm] * (2 + len(RAW)),
        out_specs=[hbm, hbm, vmem, vmem],
        scratch_shapes=[pltpu.VMEM(shape, dtype) for shape, dtype in SCRATCH.values()]
        + [pltpu.SemaphoreType.DMA(shape) for shape in SEMAPHORES.values()],
        compiler_params=pltpu.CompilerParams(
            collective_id=0, has_side_effects=True, vmem_limit_bytes=121 * 2**19
        ),
    )(task_ids, counts, latents, cotangent, *raw)
    return pl.pallas_call(
        finish,
        out_shape=[array, array] + [jax.ShapeDtypeStruct(shape, F32) for shape in SHAPES],
        in_specs=[hbm] * 4,
        out_specs=[hbm] * 10,
        scratch_shapes=[
            pltpu.VMEM((8, 256, 512), BF16),
            pltpu.VMEM((TILES, 16, 128), F32),
            pltpu.VMEM((32, 128), F32),
            *(pltpu.VMEM(shape, F32) for shape in SHAPES),
            pltpu.SemaphoreType.DMA((2, 8)),
            pltpu.SemaphoreType.DMA((2,)),
            pltpu.SemaphoreType.DMA((8,)),
        ],
    )(*found)


def body(
    latents,
    task_ids,
    slot_counts,
    cotangent,
    task_embed,
    norms,
    attn_in,
    attn_out,
    out_biases,
    mlp_in,
    mlp_in_bias,
    mlp_out,
):
    raw = (attn_in, attn_out, mlp_in, mlp_out, task_embed.T, norms, out_biases, mlp_in_bias.reshape(1, 16))
    found = list(whole(task_ids, slot_counts, latents, cotangent, *raw))
    found[2] = found[2].T
    found[8] = found[8].reshape(16)
    return tuple(found)


def solution(mesh):
    in_specs = (
        P(("dp", "fsdp"), None, None),
        P(("dp", "fsdp")),
        P(("dp", "fsdp")),
        P(("dp", "fsdp"), None, None),
        P(None, ("dp", "fsdp")),
        P(None, ("dp", "fsdp")),
        P(("dp", "fsdp"), None),
        P(("dp", "fsdp"), None),
        P(None, ("dp", "fsdp")),
        P(("dp", "fsdp"), None),
        P(("dp", "fsdp")),
        P(("dp", "fsdp"), None),
    )
    out_specs = (
        P(("dp", "fsdp"), None, None),
        P(("dp", "fsdp"), None, None),
        P(None, ("dp", "fsdp")),
        P(None, ("dp", "fsdp")),
        P(("dp", "fsdp"), None),
        P(("dp", "fsdp"), None),
        P(None, ("dp", "fsdp")),
        P(("dp", "fsdp"), None),
        P(("dp", "fsdp")),
        P(("dp", "fsdp"), None),
    )
    return jax.shard_map(body, mesh=mesh, in_specs=in_specs, out_specs=out_specs, check_vma=False)
```

profile of v0, /device:TPU:0, one launch (start us, length us, event | category | flops | bytes accessed | tf_op | source)
XLA Modules:
  0.0 96.1 jit_solution(18360968293214763797)
XLA Ops:
  0.6 92.1 %shard_map.195 = (bf16[2,512,512]{2,1,0:T(8,128)(2,1)}, bf16[2,512,512]{2,1,0:T(8,128)(2,1)}, f32[12,16,128]{2,1,0:T(8,128)}, f32[32,128]{1,0:T(8,128)}) custom-call(s32[2]{0:T(128)} %refs_0_.1, s32[2]{0:T(128)} %refs_1_.1, bf16[2,512,512]{2,1,0:T(8,128)(2,1)} %refs_2_.1, bf16[2,512,512]{2,1,0:T(8,128)(2,1)} %refs_3_.1, bf16[4,1536]{1,0:T(4,128)(2,1)} %refs_4_.1, ...), custom_call_target="tpu_custom_call" | custom-call | tf_op jit(solution)/shard_map/pallas_call | solution.py:891
  92.8 3.1 %shard_map.196 = (bf16[2,512,512]{2,1,0:T(8,128)(2,1)}, bf16[2,512,512]{2,1,0:T(8,128)(2,1)}, f32[4,18]{1,0:T(4,128)}, f32[4,4]{1,0:T(4,128)}, f32[4,1536]{1,0:T...) custom-call(bf16[2,512,512]{2,1,0:T(8,128)(2,1)} %get-tuple-element., ...), custom_call_target="tpu_custom_call" | custom-call | tf_op jit(solution)/shard_map/pallas_call | solution.py:907
where the time goes:
time: 96.2 us; the launch traced here: 96.1 us
  Pallas kernels  95.2 us (99%)
    pallas_call x1, Pallas kernels, whole(): pl.pallas_call(kernel, out_shape=[array, array, jax.ShapeDtypeStruct((TIL...  92.1 us
    pallas_call x1, Pallas kernels, whole(): pl.pallas_call(finish, out_shape=[array, array] + [jax.ShapeDtypeStruct(s...  3.1 us

commit v1 on v0

--- a/solution.py
+++ b/solution.py
@@ -696,14 +696,10 @@
         gathers[0].arrive_pair(t)
     for t in range(3):
         unfold(r, t, r.w_qkv)
-    for i in range(2):
-        project(r, i)
-
-    def forward(i):
-        for hp in range(4):
-            attend(r, i, hp)
-
-    loop(2, forward)
+    loop(2, lambda i: project(r, i))
+
+    for n in range(8):
+        attend(r, n // 4, n % 4)
     gathers[1].arrive(2)
     gathers[1].arrive_pair(0)
     unfold(r, 3, r.w_out)
@@ -744,24 +740,20 @@
         for piece in g_halves[j]:
             piece.add(1)
 
-    feed_forward(r, 0)
-
-    def middle(n):
-        feed_forward(r, n + 1)
-        chunk_gradients(r, n)
-        leave(n)
-
-        @pl.when(n > 0)
+    r.back[...] = jnp.zeros_like(r.back)
+
+    def middle(j):
+        feed_forward(r, j)
+        chunk_gradients(r, j)
+        leave(j)
+
+        @pl.when(j > 0)
         def _():
-            begin(n - 1)
-
-    loop(3, middle)
-    chunk_gradients(r, 3)
-    leave(3)
-    begin(2)
+            begin(j - 1)
+
+    loop(4, middle)
     second(0)
-    second_norm_back(r, 0)
-    second_norm_back(r, 1)
+    loop(2, lambda i: second_norm_back(r, i))
     begin(3)
     second(1)
     out_gradient(r)
@@ -805,8 +797,7 @@
     turn(g_out, 1)
     tiny_sum.add_pair()
     tiny_sum.start(0)
-    result_of(r, 0)
-    result_of(r, 1)
+    loop(2, lambda i: result_of(r, i))
     store_out.start()
     tiny_sum.add(0)
     tiny_sum.start(1)

time: 96.2 us -> 93.7 us (0.974)
  Pallas kernels: 95.2 us -> 92.6 us
    pallas_call x1, Pallas kernels: 92.1 us -> 89.5 us  [whole(): pl.pallas_call(kernel, out_shape=[array, array, jax.ShapeDtypeStruct((TIL...]
where the time goes in v1:
time: 93.7 us; the launch traced here: 93.5 us
  Pallas kernels  92.6 us (99%)
    pallas_call x1, Pallas kernels, whole(): pl.pallas_call(kernel, out_shape=[array, array, jax.ShapeDtypeStruct((TIL...  89.5 us
    pallas_call x1, Pallas kernels, whole(): pl.pallas_call(finish, out_shape=[array, array] + [jax.ShapeDtypeStruct(s...  3.1 us

profile of v1, /device:TPU:0, one launch (start us, length us, event | category | flops | bytes accessed | tf_op | source)
XLA Modules:
  0.0 93.5 jit_solution(15691150980385606289)
XLA Ops:
  0.6 89.5 %shard_map.195 = (bf16[2,512,512]{2,1,0:T(8,128)(2,1)}, bf16[2,512,512]{2,1,0:T(8,128)(2,1)}, f32[12,16,128]{2,1,0:T(8,128)}, f32[32,128]{1,0:T(8,128)}) custom-call(s32[2]{0:T(128)} %refs_0_.1, s32[2]{0:T(128)} %refs_1_.1, bf16[2,512,512]{2,1,0:T(8,128)(2,1)} %refs_2_.1, bf16[2,512,512]{2,1,0:T(8,128)(2,1)} %refs_3_.1, bf16[4,1536]{1,0:T(4,128)(2,1)} %refs_4_.1, ...), custom_call_target="tpu_custom_call" | custom-call | tf_op jit(solution)/shard_map/pallas_call | solution.py:882
  90.2 3.1 %shard_map.196 = (bf16[2,512,512]{2,1,0:T(8,128)(2,1)}, bf16[2,512,512]{2,1,0:T(8,128)(2,1)}, f32[4,18]{1,0:T(4,128)}, f32[4,4]{1,0:T(4,128)}, f32[4,1536]{1,0:T...) custom-call(bf16[2,512,512]{2,1,0:T(8,128)(2,1)} %get-tuple-element., ...), custom_call_target="tpu_custom_call" | custom-call | tf_op jit(solution)/shard_map/pallas_call | solution.py:898

commit v2 on v1

--- a/solution.py
+++ b/solution.py
@@ -459,7 +459,6 @@
     add_small(r, 20, column_sum(grad * unit))
     add_small(r, 21, column_sum(grad))
     y = r.y[i].astype(F32)
-    add_small(r, 23, column_sum(y))
     gh1 = y + normalized_back(grad, unit, r.factors[rows_of(i), 1:2], r.params[20:21])
     r.back[rows_of(i)] = gh1
     gb = gh1.astype(BF16)
@@ -684,6 +683,9 @@
     gathers[0].start(2)
     tiny.arrive(1)
     tiny.start(2)
+    loads[9].wait()
+    for i in range(2):
+        add_small(r, 23, column_sum(r.y[i].astype(F32)))
     tiny.arrive(2)
     gathers[0].arrive(2)
     gathers[1].arrive(1)
@@ -713,7 +715,6 @@
     for gather in gathers:
         gather.settle()
     tiny.settle()
-    loads[9].wait()
 
     def leave(j):
         up, down, _ = chunk(j)

time: 93.7 us -> 93.6 us (level)
  no operation moved by 1% of the time
where the time goes in v2:
time: 93.6 us; the launch traced here: 93.4 us
  Pallas kernels  92.6 us (99%)
    pallas_call x1, Pallas kernels, whole(): pl.pallas_call(kernel, out_shape=[array, array, jax.ShapeDtypeStruct((TIL...  89.5 us
    pallas_call x1, Pallas kernels, whole(): pl.pallas_call(finish, out_shape=[array, array] + [jax.ShapeDtypeStruct(s...  3.1 us

profile of v2, /device:TPU:0, one launch (start us, length us, event | category | flops | bytes accessed | tf_op | source)
XLA Modules:
  0.0 93.4 jit_solution(17142819575396257913)
XLA Ops:
  0.6 89.5 %shard_map.195 = (bf16[2,512,512]{2,1,0:T(8,128)(2,1)}, bf16[2,512,512]{2,1,0:T(8,128)(2,1)}, f32[12,16,128]{2,1,0:T(8,128)}, f32[32,128]{1,0:T(8,128)}) custom-call(s32[2]{0:T(128)} %refs_0_.1, s32[2]{0:T(128)} %refs_1_.1, bf16[2,512,512]{2,1,0:T(8,128)(2,1)} %refs_2_.1, bf16[2,512,512]{2,1,0:T(8,128)(2,1)} %refs_3_.1, bf16[4,1536]{1,0:T(4,128)(2,1)} %refs_4_.1, ...), custom_call_target="tpu_custom_call" | custom-call | tf_op jit(solution)/shard_map/pallas_call | solution.py:883
  90.2 3.1 %shard_map.196 = (bf16[2,512,512]{2,1,0:T(8,128)(2,1)}, bf16[2,512,512]{2,1,0:T(8,128)(2,1)}, f32[4,18]{1,0:T(4,128)}, f32[4,4]{1,0:T(4,128)}, f32[4,1536]{1,0:T...) custom-call(bf16[2,512,512]{2,1,0:T(8,128)(2,1)} %get-tuple-element., ...), custom_call_target="tpu_custom_call" | custom-call | tf_op jit(solution)/shard_map/pallas_call | solution.py:899

commit v3 on v2

--- a/solution.py
+++ b/solution.py
@@ -287,7 +287,7 @@
 
 def unfold(r, t, out):
     blocks = [r.tiles[t, xc // 2, xc % 2].reshape(256, 128) for xc in range(8)]
-    rows = nn(quarter_order(), jnp.concatenate(blocks, 1)).astype(jnp.bfloat16)
+    rows = nn(r.orders[0], jnp.concatenate(blocks, 1)).astype(jnp.bfloat16)
     for q, ct in enumerate(COLUMNS[t]):
         for xc in range(8):
             out[xc * 64 : (xc + 1) * 64, ct * 128 : (ct + 1) * 128] = rows[q * 64 : (q + 1) * 64, xc * 128 : (xc + 1) * 128]
@@ -304,7 +304,7 @@
 
 def fold(r, columns, t):
     rows = [jnp.concatenate([block[xc * 64 : (xc + 1) * 64] for xc in range(8)], 1) for block in columns]
-    blocks = nn(quarter_order(True), jnp.concatenate(rows, 0)).astype(jnp.bfloat16)
+    blocks = nn(r.orders[1], jnp.concatenate(rows, 0)).astype(jnp.bfloat16)
     for xc in range(8):
         r.tiles[t, xc // 2, xc % 2] = blocks[:, xc * 128 : (xc + 1) * 128].reshape(4, 4, 16, 128)
 
@@ -551,6 +551,7 @@
     "small32": ((40, 128), F32),
     "table32": ((128, 128), F32),
     "own_small": ((32, 128), BF16),
+    "orders": ((2, 256, 256), BF16),
     "lat": ((2, 512, 512), BF16),
     "y": ((2, 512, 512), BF16),
     "w_qkv": ((512, 1536), BF16),
@@ -683,6 +684,8 @@
     gathers[0].start(2)
     tiny.arrive(1)
     tiny.start(2)
+    r.orders[0] = quarter_order()
+    r.orders[1] = quarter_order(True)
     loads[9].wait()
     for i in range(2):
         add_small(r, 23, column_sum(r.y[i].astype(F32)))

time: 93.6 us -> 93.7 us (level)
  no operation moved by 1% of the time
where the time goes in v3:
time: 93.7 us; the launch traced here: 93.5 us
  Pallas kernels  92.6 us (99%)
    pallas_call x1, Pallas kernels, whole(): pl.pallas_call(kernel, out_shape=[array, array, jax.ShapeDtypeStruct((TIL...  89.5 us
    pallas_call x1, Pallas kernels, whole(): pl.pallas_call(finish, out_shape=[array, array] + [jax.ShapeDtypeStruct(s...  3.1 us

profile of v3, /device:TPU:0, one launch (start us, length us, event | category | flops | bytes accessed | tf_op | source)
XLA Modules:
  0.0 93.5 jit_solution(6863816875462160032)
XLA Ops:
  0.6 89.5 %shard_map.195 = (bf16[2,512,512]{2,1,0:T(8,128)(2,1)}, bf16[2,512,512]{2,1,0:T(8,128)(2,1)}, f32[12,16,128]{2,1,0:T(8,128)}, f32[32,128]{1,0:T(8,128)}) custom-call(s32[2]{0:T(128)} %refs_0_.1, s32[2]{0:T(128)} %refs_1_.1, bf16[2,512,512]{2,1,0:T(8,128)(2,1)} %refs_2_.1, bf16[2,512,512]{2,1,0:T(8,128)(2,1)} %refs_3_.1, bf16[4,1536]{1,0:T(4,128)(2,1)} %refs_4_.1, ...), custom_call_target="tpu_custom_call" | custom-call | tf_op jit(solution)/shard_map/pallas_call | solution.py:886
  90.2 3.1 %shard_map.196 = (bf16[2,512,512]{2,1,0:T(8,128)(2,1)}, bf16[2,512,512]{2,1,0:T(8,128)(2,1)}, f32[4,18]{1,0:T(4,128)}, f32[4,4]{1,0:T(4,128)}, f32[4,1536]{1,0:T...) custom-call(bf16[2,512,512]{2,1,0:T(8,128)(2,1)} %get-tuple-element., ...), custom_call_target="tpu_custom_call" | custom-call | tf_op jit(solution)/shard_map/pallas_call | solution.py:902

commit v4 on v3

--- a/solution.py
+++ b/solution.py
@@ -848,6 +848,9 @@
             writes.append(pltpu.make_async_copy(held.at[slot], target.at[k // 2, rows], sems.at[1, slot]))
     for read in reads:
         read.start()
+    for n in range(4):
+        reads[n].wait()
+        writes[n].start()
     for load in loads:
         load.wait()
     for t, blocks in enumerate(COLUMNS):
@@ -871,9 +874,9 @@
     ]
     for store in stores:
         store.start()
-    for read, write in zip(reads, writes, strict=True):
-        read.wait()
-        write.start()
+    for n in range(4, 8):
+        reads[n].wait()
+        writes[n].start()
     for copy in (*stores, *writes):
         copy.wait()
 

time: 93.7 us -> 93.3 us (level)
  no operation moved by 1% of the time
where the time goes in v4:
time: 93.3 us; the launch traced here: 93.1 us
  Pallas kernels  92.3 us (99%)
    pallas_call x1, Pallas kernels, whole(): pl.pallas_call(kernel, out_shape=[array, array, jax.ShapeDtypeStruct((TIL...  89.5 us
    pallas_call x1, Pallas kernels, whole(): pl.pallas_call(finish, out_shape=[array, array] + [jax.ShapeDtypeStruct(s...  2.76 us

profile of v4, /device:TPU:0, one launch (start us, length us, event | category | flops | bytes accessed | tf_op | source)
XLA Modules:
  0.0 93.1 jit_solution(17982699855034170284)
XLA Ops:
  0.6 89.5 %shard_map.195 = (bf16[2,512,512]{2,1,0:T(8,128)(2,1)}, bf16[2,512,512]{2,1,0:T(8,128)(2,1)}, f32[12,16,128]{2,1,0:T(8,128)}, f32[32,128]{1,0:T(8,128)}) custom-call(s32[2]{0:T(128)} %refs_0_.1, s32[2]{0:T(128)} %refs_1_.1, bf16[2,512,512]{2,1,0:T(8,128)(2,1)} %refs_2_.1, bf16[2,512,512]{2,1,0:T(8,128)(2,1)} %refs_3_.1, bf16[4,1536]{1,0:T(4,128)(2,1)} %refs_4_.1, ...), custom_call_target="tpu_custom_call" | custom-call | tf_op jit(solution)/shard_map/pallas_call | solution.py:889
  90.2 2.8 %shard_map.196 = (bf16[2,512,512]{2,1,0:T(8,128)(2,1)}, bf16[2,512,512]{2,1,0:T(8,128)(2,1)}, f32[4,18]{1,0:T(4,128)}, f32[4,4]{1,0:T(4,128)}, f32[4,1536]{1,0:T...) custom-call(bf16[2,512,512]{2,1,0:T(8,128)(2,1)} %get-tuple-element., ...), custom_call_target="tpu_custom_call" | custom-call | tf_op jit(solution)/shard_map/pallas_call | solution.py:905
